TPU v7x, 256 devices: a whole 4x4x8 slice. The times are simulated.
256 devices in a mesh: dp: 16 (over z, core), tensor: 16 (over y, x).
Axes of the slice: x: 4, y: 4, z: 8, core: 2. Of those that a mesh axis runs over, the one named last changes fastest.
Arguments:
- queries: bfloat16 [64, 256, 8192], P('dp', None, 'tensor'), may hold values from -5 to 5
- grad_output: bfloat16 [64, 256, 8192], P('dp', None, 'tensor'), may hold values from -5 to 5
- image_keys: bfloat16 [16, 256, 256, 128], P('tensor', 'dp'), may hold values from -5 to 5
- image_values: bfloat16 [16, 256, 256, 128], P('tensor', 'dp'), may hold values from -5 to 5
- attn_gate: float32 [1], replicated, may hold values from 0.3 to 1.2
- image_counts: int32 [64], P('dp'), may hold values from 1 to 4
- text_lengths: int32 [64], P('dp'), may hold values from 64 to 256
- tile_owner: int32 [64, 4], P('dp'), may hold values from 0 to 15, as said below
Outputs:
- grad_queries: bfloat16 [64, 256, 8192], P('dp', None, 'tensor')
- grad_keys: bfloat16 [16, 256, 256, 128], P('tensor', 'dp')
- grad_values: bfloat16 [16, 256, 256, 128], P('tensor', 'dp')
Inputs may be any that keep to these rules, and one draw needn't show every extreme that they name: `tile_owner`: for each index g along dp, the 16 tiles of its samples name every index along dp exactly once.
All inputs are finite; a program needn't handle non-finite values.
Results may differ from a plain program's by a relative error of at most 0.03.
Values may be sent and summed in bfloat16 or wider, within the bound.
A program may use at most 128 MiB of HBM per device.

v0:
```python
import jax
import jax.numpy as jnp
from jax import lax
from jax.sharding import PartitionSpec as P

masked_score = -1e30


def swapped(block, axis, apart):
    count = lax.axis_size(axis)
    route = []
    for low in range(count):
        high = low | 1 << apart
        if high != low and high < count:
            route += [(low, high), (high, low)]
    return lax.ppermute(block, axis, route)


def tile_order(pair_bit, own_half, other_half):
    joined_low = jnp.concatenate((own_half, other_half), 2)
    joined_high = jnp.concatenate((other_half, own_half), 2)
    return jnp.where(pair_bit == 0, joined_low, joined_high)[0]


def shards(
    queries,
    grad_output,
    image_keys,
    image_values,
    attn_gate,
    image_counts,
    text_lengths,
    tile_owner,
):
    sample_count, text_rows, row_width = queries.shape
    head_dim = image_keys.shape[3]
    half_tile = image_keys.shape[2]
    tile_rows = 2 * half_tile
    head_count = row_width // head_dim
    tile_slots = tile_owner.shape[1]
    key_count = tile_slots * tile_rows
    score_scale = head_dim ** (-0.5)
    pair_bit = lax.axis_index("tensor") % 2
    tile_live = jnp.arange(tile_slots)[None, :] < image_counts[:, None]
    row_live = (jnp.arange(text_rows)[None, :] < text_lengths[:, None]).astype(jnp.float32)
    gate_gain = jnp.tanh(attn_gate[0])
    grad_rows = (gate_gain * grad_output.astype(jnp.float32) * row_live[:, :, None]).astype(
        jnp.bfloat16
    )
    slot_order = jnp.argsort(tile_owner.reshape(-1))
    keys_here, values_here = (
        lax.all_to_all(image_keys, "dp", split_axis=1, concat_axis=1, tiled=True),
        lax.all_to_all(image_values, "dp", split_axis=1, concat_axis=1, tiled=True),
    )
    keys_pair, values_pair = swapped((keys_here, values_here), "tensor", 0)
    key_tiles = tile_order(pair_bit, keys_here, keys_pair)
    value_tiles = tile_order(pair_bit, values_here, values_pair)
    sample_keys = key_tiles[tile_owner].reshape(sample_count, key_count, head_dim)
    sample_values = value_tiles[tile_owner].reshape(sample_count, key_count, head_dim)
    key_live = jnp.repeat(tile_live, tile_rows, axis=1)

    def per_sample(sample_items):
        query, grad, key_rows, value_rows, live = sample_items
        query_heads = query.reshape(text_rows, head_count, head_dim)
        grad_heads = grad.reshape(text_rows, head_count, head_dim)
        scores = (
            jnp.einsum("thd,kd->htk", query_heads, key_rows, preferred_element_type=jnp.float32)
            * score_scale
        )
        scores = jnp.where(live[None, None, :], scores, masked_score)
        row_top = jnp.max(scores, axis=-1, keepdims=True)
        exponent = jnp.exp(scores - row_top)
        weights = exponent / jnp.sum(exponent, axis=-1, keepdims=True)
        grad_weights = jnp.einsum(
            "thd,kd->htk", grad_heads, value_rows, preferred_element_type=jnp.float32
        )
        row_delta = jnp.sum(weights * grad_weights, axis=-1, keepdims=True)
        grad_scores = (weights * (grad_weights - row_delta)).astype(jnp.bfloat16)
        weights_low = weights.astype(jnp.bfloat16)
        query_grad = (
            jnp.einsum("htk,kd->thd", grad_scores, key_rows, preferred_element_type=jnp.float32)
            * score_scale
        )
        key_grad = (
            jnp.einsum("htk,thd->kd", grad_scores, query_heads, preferred_element_type=jnp.float32)
            * score_scale
        )
        value_grad = jnp.einsum(
            "htk,thd->kd", weights_low, grad_heads, preferred_element_type=jnp.float32
        )
        return (
            query_grad.astype(jnp.bfloat16).reshape(text_rows, row_width),
            key_grad.astype(jnp.bfloat16),
            value_grad.astype(jnp.bfloat16),
        )

    grad_queries, key_parts, value_parts = lax.map(
        per_sample, (queries, grad_rows, sample_keys, sample_values, key_live)
    )
    key_owned = key_parts.reshape(sample_count * tile_slots, tile_rows, head_dim)[slot_order]
    value_owned = value_parts.reshape(sample_count * tile_slots, tile_rows, head_dim)[slot_order]

    def take_half(block, which):
        return lax.dynamic_slice_in_dim(block, which * half_tile, half_tile, 1)

    key_home, value_home = (
        lax.all_to_all(key_owned, "dp", split_axis=0, concat_axis=0, tiled=True),
        lax.all_to_all(value_owned, "dp", split_axis=0, concat_axis=0, tiled=True),
    )
    key_mine = take_half(key_home, pair_bit)
    value_mine = take_half(value_home, pair_bit)
    key_give = take_half(key_home, 1 - pair_bit)
    value_give = take_half(value_home, 1 - pair_bit)
    key_got, value_got = swapped((key_give, value_give), "tensor", 0)
    key_total = (key_mine.astype(jnp.float32) + key_got.astype(jnp.float32)).astype(jnp.bfloat16)
    value_total = (value_mine.astype(jnp.float32) + value_got.astype(jnp.float32)).astype(
        jnp.bfloat16
    )
    return (grad_queries, key_total[None], value_total[None])


def solution(mesh):
    return jax.shard_map(
        shards,
        mesh=mesh,
        in_specs=(
            P("dp", None, "tensor"),
            P("dp", None, "tensor"),
            P("tensor", "dp", None, None),
            P("tensor", "dp", None, None),
            P(),
            P("dp"),
            P("dp"),
            P("dp", None),
        ),
        out_specs=(
            P("dp", None, "tensor"),
            P("tensor", "dp", None, None),
            P("tensor", "dp", None, None),
        ),
        check_vma=False,
    )
```

profile of v0, /device:TPU:40, one launch (start us, length us, event | category | flops | bytes accessed | tf_op | source)
XLA Modules:
  0.0 329.5 jit_solution(788206051841448645)
XLA Ops:
  0.7 34.2 %all_to_all.20 = bf16[1,16,256,128]{3,2,0,1:T(8,128)(2,1)S(1)} all-to-all(bf16[1,16,256,128]{3,2,0,1:T(8,128)(2,1)} %bitcast.151), channel_id=1, replica_groups=mesh['dp'=16,'tensor'=16] {'dp'}, dimensions={1} | all-to-all | bytes 2097152 | tf_op jit(solution)/shard_map/all_to_all | solution.py:53
  34.8 6.0 %all-to-all-start = ((bf16[1,16,256,128]{3,2,0,1:T(8,128)(2,1)}), bf16[1,16,256,128]{3,2,0,1:T(8,128)(2,1)S(1)}, u32[]{:S(2)}, u32[]{:S(2)}) async-start(bf16[1,16,256,128]{3,2,0,1:T(8,128)(2,1)} %bitcast.15), calls=%async_computation | async-start | bytes 2097152 | tf_op jit(solution)/shard_map/all_to_all | solution.py:52
  41.0 1.5 collective-permute-start.1
  42.5 23.1 %all-to-all-done = bf16[1,16,256,128]{3,2,0,1:T(8,128)(2,1)S(1)} async-done(((bf16[1,16,256,128]{3,2,0,1:T(8,128)(2,1)}), bf16[1,16,256,128]{3,2,0,1:T(8,128)(2,1)S(1)}, u32[]{:S(2)}, u32[]{:S(2)}) %all-to-all-start) | async-done | bytes 1048608 | tf_op jit(solution)/shard_map/all_to_all | solution.py:52
  65.6 1.5 collective-permute-start
  68.0 1.5 copy.32
  69.5 1.2 sort.17
  71.4 1.2 multiply_convert_fusion
  72.6 18.8 %collective-permute-done = bf16[1,16,256,128]{3,2,0,1:T(8,128)(2,1)} collective-permute-done((bf16[1,16,256,128]{3,2,0,1:T(8,128)(2,1)S(1)}, bf16[1,16,256,128]{3,2,0,1:T(8,128)(2,1)}, u32[]{:S(2)}, u32[]{:S(2)}) %collective-permute-start) | collective-permute-done | bytes 1048608 | tf_op jit(solution)/shard_map/ppermute | solution.py:16
  91.5 4.6 %maximum_select_fusion = (bf16[16,512,128]{2,1,0:T(8,128)(2,1)}, bf16[16,512,128]{2,1,0:T(8,128)(2,1)}) fusion(bf16[16,256,128]{2,1,0:T(8,128)(2,1)} %bitcast.17, bf16[16,256,128]{2,1,0:T(8,128)(2,1)S(1)} %bitcast.147, pred[]{:T(512)S(6)} %eq.6, bf16[16,256,128]{2,1,0:T(8,128)(2,1)S(1)} %bitcast.146, bf16[16,256,128]{2,1,0:T(8,128)(2,1)} %bitcast.22), kind=kLoop, calls=%fused_computation.53 | loop fusion | flops 18874368 | bytes 8388609 | tf_op jit(solution)/shard_map/jit(_where)/select_n | solution.py:22
  96.0 2.5 gather_fusion
  98.6 3.8 %gather_fusion.1 = bf16[16,512,128]{2,1,0:T(8,128)(2,1)} fusion(bf16[16,512,128]{2,1,0:T(8,128)(2,1)} %get-tuple-element.107, s32[1024]{0:T(1024)S(1)} %pad_clamp_fusion.1), kind=kCustom, calls=%fused_computation.1 | custom fusion | bytes 4194368 | tf_op jit(solution)/shard_map/gather | solution.py:59
  102.4 84.6 %while.14 = (s32[]{:T(128)}, bf16[4,256,512]{2,1,0:T(8,128)(2,1)}, bf16[4,2048,128]{2,1,0:T(8,128)(2,1)}, bf16[4,2048,128]{2,1,0:T(8,128)(2,1)}, bf16[4,2048,128...) while((s32[]{:T(128)}, bf16[4,256,512]{2,1,0:T(8,128)(2,1)}, ...), condition=%wide.region_4.5_spmd, body=%wide.region_0.4_spmd.sunk | while | flops 2712667136 | bytes 103053464 | solution.py:97
  103.4 1.0 constant_dynamic-slice_fusion.6
  104.5 6.0 %fusion.95 = (f32[4,256]{1,0:T(4,128)S(1)}, f32[4,256,2048]{1,2,0:T(8,128)}) fusion(pred[2048]{0:T(1024)(128)(4,1)S(1)} %dynamic-slice_reduce_fusion.2, bf16[256,4,128]{0,2,1:T(8,128)(2,1)S(1)} %bitcast.143, bf16[4,2048,128]{2,1,0:T(8,128)(2,1)S(1)} %get-tuple-element.195, s32[]{:T(128)S(6)} %copy.57), kind=kOutput, calls=%fused_computation.70.clone.1 | convolution fusion | flops 545261568 | bytes 9181188 | tf_op jit(solution)/shard_map/while/body/eval_jaxpr/sub | solution.py:72
  110.5 5.6 %fusion.100 = bf16[4,2048,128]{2,1,0:T(8,128)(2,1)} fusion(bf16[4,2048,128]{2,1,0:T(8,128)(2,1)} %get-tuple-element.184, s32[]{:T(128)S(6)} %copy.57, bf16[256,4,128]{0,2,1:T(8,128)(2,1)S(1)} %bitcast.141, f32[4,256,2048]{1,2,0:T(8,128)} %get-tuple-element.167, f32[4,256]{1,0:T(4,128)S(1)} %get-tuple-element.168), kind=kOutput, calls=%fused_computation.29.clone.1 | convolution fusion | flops 541327360 | bytes 9179140 | tf_op jit(solution)/shard_map/while/body/eval_jaxpr/htk,thd->kd/dot_general | solution.py:88
  116.2 2.3 fusion.96
  118.6 1.2 fusion.97
  120.5 2.1 fusion.99
  124.5 1.0 constant_dynamic-slice_fusion.6
  125.7 6.0 %fusion.95 = (f32[4,256]{1,0:T(4,128)S(1)}, f32[4,256,2048]{1,2,0:T(8,128)}) fusion(pred[2048]{0:T(1024)(128)(4,1)S(1)} %dynamic-slice_reduce_fusion.2, bf16[256,4,128]{0,2,1:T(8,128)(2,1)S(1)} %bitcast.143, bf16[4,2048,128]{2,1,0:T(8,128)(2,1)S(1)} %get-tuple-element.195, s32[]{:T(128)S(6)} %copy.57), kind=kOutput, calls=%fused_computation.70.clone.1 | convolution fusion | flops 545261568 | bytes 9181188 | tf_op jit(solution)/shard_map/while/body/eval_jaxpr/sub | solution.py:72
  131.6 5.6 %fusion.100 = bf16[4,2048,128]{2,1,0:T(8,128)(2,1)} fusion(bf16[4,2048,128]{2,1,0:T(8,128)(2,1)} %get-tuple-element.184, s32[]{:T(128)S(6)} %copy.57, bf16[256,4,128]{0,2,1:T(8,128)(2,1)S(1)} %bitcast.141, f32[4,256,2048]{1,2,0:T(8,128)} %get-tuple-element.167, f32[4,256]{1,0:T(4,128)S(1)} %get-tuple-element.168), kind=kOutput, calls=%fused_computation.29.clone.1 | convolution fusion | flops 541327360 | bytes 9179140 | tf_op jit(solution)/shard_map/while/body/eval_jaxpr/htk,thd->kd/dot_general | solution.py:88
  137.4 2.3 fusion.96
  139.7 1.2 fusion.97
  141.7 2.1 fusion.99
  146.8 6.0 %fusion.95 = (f32[4,256]{1,0:T(4,128)S(1)}, f32[4,256,2048]{1,2,0:T(8,128)}) fusion(pred[2048]{0:T(1024)(128)(4,1)S(1)} %dynamic-slice_reduce_fusion.2, bf16[256,4,128]{0,2,1:T(8,128)(2,1)S(1)} %bitcast.143, bf16[4,2048,128]{2,1,0:T(8,128)(2,1)S(1)} %get-tuple-element.195, s32[]{:T(128)S(6)} %copy.57), kind=kOutput, calls=%fused_computation.70.clone.1 | convolution fusion | flops 545261568 | bytes 9181188 | tf_op jit(solution)/shard_map/while/body/eval_jaxpr/sub | solution.py:72
  152.8 5.6 %fusion.100 = bf16[4,2048,128]{2,1,0:T(8,128)(2,1)} fusion(bf16[4,2048,128]{2,1,0:T(8,128)(2,1)} %get-tuple-element.184, s32[]{:T(128)S(6)} %copy.57, bf16[256,4,128]{0,2,1:T(8,128)(2,1)S(1)} %bitcast.141, f32[4,256,2048]{1,2,0:T(8,128)} %get-tuple-element.167, f32[4,256]{1,0:T(4,128)S(1)} %get-tuple-element.168), kind=kOutput, calls=%fused_computation.29.clone.1 | convolution fusion | flops 541327360 | bytes 9179140 | tf_op jit(solution)/shard_map/while/body/eval_jaxpr/htk,thd->kd/dot_general | solution.py:88
  158.5 2.3 fusion.96
  160.9 1.2 fusion.97
  162.8 2.1 fusion.99
  166.8 1.0 constant_dynamic-slice_fusion.6
  167.9 6.0 %fusion.95 = (f32[4,256]{1,0:T(4,128)S(1)}, f32[4,256,2048]{1,2,0:T(8,128)}) fusion(pred[2048]{0:T(1024)(128)(4,1)S(1)} %dynamic-slice_reduce_fusion.2, bf16[256,4,128]{0,2,1:T(8,128)(2,1)S(1)} %bitcast.143, bf16[4,2048,128]{2,1,0:T(8,128)(2,1)S(1)} %get-tuple-element.195, s32[]{:T(128)S(6)} %copy.57), kind=kOutput, calls=%fused_computation.70.clone.1 | convolution fusion | flops 545261568 | bytes 9181188 | tf_op jit(solution)/shard_map/while/body/eval_jaxpr/sub | solution.py:72
  173.9 5.6 %fusion.100 = bf16[4,2048,128]{2,1,0:T(8,128)(2,1)} fusion(bf16[4,2048,128]{2,1,0:T(8,128)(2,1)} %get-tuple-element.184, s32[]{:T(128)S(6)} %copy.57, bf16[256,4,128]{0,2,1:T(8,128)(2,1)S(1)} %bitcast.141, f32[4,256,2048]{1,2,0:T(8,128)} %get-tuple-element.167, f32[4,256]{1,0:T(4,128)S(1)} %get-tuple-element.168), kind=kOutput, calls=%fused_computation.29.clone.1 | convolution fusion | flops 541327360 | bytes 9179140 | tf_op jit(solution)/shard_map/while/body/eval_jaxpr/htk,thd->kd/dot_general | solution.py:88
  179.7 2.3 fusion.96
  182.0 1.2 fusion.97
  184.0 2.1 fusion.99
  186.9 3.9 %gather_fusion.2 = bf16[16,512,128]{2,1,0:T(8,128)(2,1)} fusion(bf16[16,512,128]{2,1,0:T(8,128)(2,1)} %bitcast.149, s32[1024]{0:T(1024)} %pad_clamp_fusion), kind=kCustom, calls=%fused_computation.2 | custom fusion | bytes 4194368 | tf_op jit(solution)/shard_map/gather | solution.py:100
  190.8 6.5 %all-to-all-start.2 = ((bf16[16,512,128]{2,1,0:T(8,128)(2,1)}), bf16[16,512,128]{2,1,0:T(8,128)(2,1)S(1)}, u32[]{:S(2)}, u32[]{:S(2)}) async-start(bf16[16,512,128]{2,1,0:T(8,128)(2,1)} %gather_fusion.2), calls=%async_computation.2 | async-start | bytes 4194304 | tf_op jit(solution)/shard_map/all_to_all | solution.py:107
  197.3 3.8 %gather_fusion.3 = bf16[16,512,128]{2,1,0:T(8,128)(2,1)} fusion(bf16[16,512,128]{2,1,0:T(8,128)(2,1)} %bitcast.148, s32[1024]{0:T(1024)} %pad_clamp_fusion), kind=kCustom, calls=%fused_computation.3 | custom fusion | bytes 4194368 | tf_op jit(solution)/shard_map/gather | solution.py:101
  201.1 43.6 %all-to-all-done.2 = bf16[16,512,128]{2,1,0:T(8,128)(2,1)S(1)} async-done(((bf16[16,512,128]{2,1,0:T(8,128)(2,1)}), bf16[16,512,128]{2,1,0:T(8,128)(2,1)S(1)}, u32[]{:S(2)}, u32[]{:S(2)}) %all-to-all-start.2) | async-done | bytes 2097184 | tf_op jit(solution)/shard_map/all_to_all | solution.py:107
  244.7 6.5 %all-to-all-start.3 = ((bf16[16,512,128]{2,1,0:T(8,128)(2,1)}), bf16[16,512,128]{2,1,0:T(8,128)(2,1)}, u32[]{:S(2)}, u32[]{:S(2)}) async-start(bf16[16,512,128]{2,1,0:T(8,128)(2,1)} %gather_fusion.3), calls=%async_computation.3 | async-start | bytes 4194304 | tf_op jit(solution)/shard_map/all_to_all | solution.py:108
  251.3 1.6 collective-permute-start.2
  252.9 45.8 %all-to-all-done.3 = bf16[16,512,128]{2,1,0:T(8,128)(2,1)} async-done(((bf16[16,512,128]{2,1,0:T(8,128)(2,1)}), bf16[16,512,128]{2,1,0:T(8,128)(2,1)}, u32[]{:S(2)}, u32[]{:S(2)}) %all-to-all-start.3) | async-done | bytes 2097184 | tf_op jit(solution)/shard_map/all_to_all | solution.py:108
  298.7 2.3 constant_dynamic-slice_fusion.2
  301.0 1.5 collective-permute-start.3
  302.5 2.5 fusion.56
  304.9 21.7 %collective-permute-done.3 = bf16[16,256,128]{2,1,0:T(8,128)(2,1)} collective-permute-done((bf16[16,256,128]{2,1,0:T(8,128)(2,1)}, bf16[16,256,128]{2,1,0:T(8,128)(2,1)}, u32[]{:S(2)}, u32[]{:S(2)}) %collective-permute-start.3) | collective-permute-done | bytes 1048608 | tf_op jit(solution)/shard_map/ppermute | solution.py:16
  326.7 2.8 fusion.57
  (56 shorter events, 13.9 us)
Async XLA Ops:
  0.6 40.2 %copy-start.3 = (s32[4]{0:T(128)S(1)}, s32[4]{0:T(128)}, u32[]{:S(2)}) copy-start(s32[4]{0:T(128)} %param.15) | copy-start | bytes 52
  0.6 66.4 %copy-start.1 = (s32[4,4]{1,0:T(4,128)S(1)}, s32[4,4]{1,0:T(4,128)}, u32[]{:S(2)}) copy-start(s32[4,4]{1,0:T(4,128)} %param.17) | copy-start | bytes 196
  34.8 36.5 %copy-start.2 = (s32[4]{0:T(128)S(1)}, s32[4]{0:T(128)}, u32[]{:S(2)}) copy-start(s32[4]{0:T(128)} %param.16) | copy-start | bytes 52
  34.8 30.7 %all-to-all-start = ((bf16[1,16,256,128]{3,2,0,1:T(8,128)(2,1)}), bf16[1,16,256,128]{3,2,0,1:T(8,128)(2,1)S(1)}, u32[]{:S(2)}, u32[]{:S(2)}) async-start(bf16[1,16,256,128]{3,2,0,1:T(8,128)(2,1)} %bitcast.15), calls=%async_computation | async-start | bytes 2097152 | tf_op jit(solution)/shard_map/all_to_all | solution.py:52
  41.0 31.6 %collective-permute-start.1 = (bf16[1,16,256,128]{3,2,1,0:T(8,128)(2,1)S(1)}, bf16[1,16,256,128]{3,2,1,0:T(8,128)(2,1)}, u32[]{:S(2)}, u32[]{:S(2)}) collective-permute-start(bf16[1,16,256,128]{3,2,1,0:T(8,128)(2,1)S(1)} %bitcast.145), channel_id=1, source_target_pairs={{0,1},{1,0},{2,3},{3,2},{4,5},{5,4},{6,7},{7,6},{8,9},{9,8},{10,11... | collective-permute-start | bytes 3145736 | tf_op jit(solution)/shard_map/ppermute | solution.py:16
  65.6 25.9 %collective-permute-start = (bf16[1,16,256,128]{3,2,0,1:T(8,128)(2,1)S(1)}, bf16[1,16,256,128]{3,2,0,1:T(8,128)(2,1)}, u32[]{:S(2)}, u32[]{:S(2)}) collective-permute-start(bf16[1,16,256,128]{3,2,0,1:T(8,128)(2,1)S(1)} %all-to-all-done), channel_id=1, source_target_pairs={{0,1},{1,0},{2,3},{3,2},{4,5},{5,4},{6,7},{7,6},{8,9},{9,8},{10,11... | collective-permute-start | bytes 3145736 | tf_op jit(solution)/shard_map/ppermute | solution.py:16
  110.5 5.8 %copy-start = (f32[4,256,2048]{1,2,0:T(8,128)S(1)}, f32[4,256,2048]{1,2,0:T(8,128)}, u32[]{:S(2)}) copy-start(f32[4,256,2048]{1,2,0:T(8,128)} %get-tuple-element.167) | copy-start | bytes 25165828 | tf_op jit(solution)/shard_map/while
  131.6 5.8 %copy-start = (f32[4,256,2048]{1,2,0:T(8,128)S(1)}, f32[4,256,2048]{1,2,0:T(8,128)}, u32[]{:S(2)}) copy-start(f32[4,256,2048]{1,2,0:T(8,128)} %get-tuple-element.167) | copy-start | bytes 25165828 | tf_op jit(solution)/shard_map/while
  152.8 5.8 %copy-start = (f32[4,256,2048]{1,2,0:T(8,128)S(1)}, f32[4,256,2048]{1,2,0:T(8,128)}, u32[]{:S(2)}) copy-start(f32[4,256,2048]{1,2,0:T(8,128)} %get-tuple-element.167) | copy-start | bytes 25165828 | tf_op jit(solution)/shard_map/while
  173.9 5.8 %copy-start = (f32[4,256,2048]{1,2,0:T(8,128)S(1)}, f32[4,256,2048]{1,2,0:T(8,128)}, u32[]{:S(2)}) copy-start(f32[4,256,2048]{1,2,0:T(8,128)} %get-tuple-element.167) | copy-start | bytes 25165828 | tf_op jit(solution)/shard_map/while
  190.8 53.8 %all-to-all-start.2 = ((bf16[16,512,128]{2,1,0:T(8,128)(2,1)}), bf16[16,512,128]{2,1,0:T(8,128)(2,1)S(1)}, u32[]{:S(2)}, u32[]{:S(2)}) async-start(bf16[16,512,128]{2,1,0:T(8,128)(2,1)} %gather_fusion.2), calls=%async_computation.2 | async-start | bytes 4194304 | tf_op jit(solution)/shard_map/all_to_all | solution.py:107
  244.7 54.0 %all-to-all-start.3 = ((bf16[16,512,128]{2,1,0:T(8,128)(2,1)}), bf16[16,512,128]{2,1,0:T(8,128)(2,1)}, u32[]{:S(2)}, u32[]{:S(2)}) async-start(bf16[16,512,128]{2,1,0:T(8,128)(2,1)} %gather_fusion.3), calls=%async_computation.3 | async-start | bytes 4194304 | tf_op jit(solution)/shard_map/all_to_all | solution.py:108
  251.3 51.2 %collective-permute-start.2 = (bf16[16,256,128]{2,1,0:T(8,128)(2,1)S(1)}, bf16[16,256,128]{2,1,0:T(8,128)(2,1)}, u32[]{:S(2)}, u32[]{:S(2)}) collective-permute-start(bf16[16,256,128]{2,1,0:T(8,128)(2,1)S(1)} %constant_dynamic-slice_fusion.3), channel_id=1, source_target_pairs={{0,1},{1,0},{2,3},{3,2},{4,5},{5,4},{6,7},{7,6},{8,9},{9,8},{10,11... | collective-permute-start | bytes 3145736 | tf_op jit(solution)/shard_map/ppermute | solution.py:16
  301.0 25.7 %collective-permute-start.3 = (bf16[16,256,128]{2,1,0:T(8,128)(2,1)}, bf16[16,256,128]{2,1,0:T(8,128)(2,1)}, u32[]{:S(2)}, u32[]{:S(2)}) collective-permute-start(bf16[16,256,128]{2,1,0:T(8,128)(2,1)} %constant_dynamic-slice_fusion.2), channel_id=1, source_target_pairs={{0,1},{1,0},{2,3},{3,2},{4,5},{5,4},{6,7},{7,6},{8,9},{9,8},{10,11... | collective-permute-start | bytes 3145736 | tf_op jit(solution)/shard_map/ppermute | solution.py:16
where the time goes:
time: 333 us; the launch traced here: 329 us
  waiting for transfers between devices  153 us (46%)
  matrix products  67.1 us (20%)
  blocking collectives  34.2 us (10%)
  local copies, waits for them, and re-layouts  30.8 us (9%)
  starting transfers between devices  25 us (8%)
  other arithmetic  17.7 us (5%)
    all_to_all x1, waiting for transfers between devices, shards(): lax.all_to_all(value_owned, 'dp', split_axis=0, concat_axis=0, tiled=True)  45.8 us
    all_to_all x1, waiting for transfers between devices, shards(): lax.all_to_all(key_owned, 'dp', split_axis=0, concat_axis=0, tiled=True)  43.6 us
    ppermute x4, waiting for transfers between devices, swapped(): return lax.ppermute(block, axis, route)  40.6 us
    all_to_all x1, blocking collectives, shards(): lax.all_to_all(image_values, 'dp', split_axis=1, concat_axis=1, tiled=True)  34.2 us
    sub x4, matrix products, per_sample(): exponent = jnp.exp(scores - row_top)  23.9 us
    all_to_all x1, waiting for transfers between devices, shards(): lax.all_to_all(image_keys, 'dp', split_axis=1, concat_axis=1, tiled=True)  23.1 us
    dot_general x4, matrix products, per_sample(): jnp.einsum('htk,thd->kd', weights_low, grad_heads, preferred_element_type...  22.4 us
    dot_general x4, matrix products, per_sample(): jnp.einsum('thd,kd->htk', grad_heads, value_rows, preferred_element_type=...  9.26 us
  transfers between devices with their start and end apart: 7, of which 5 were waited for; matrix products, arithmetic and copies ran while one was open for 4% of the time, Pallas kernels for 0%

commit v1 on v0

v1 whole, which is shorter than its diff:
```python
import functools
import math

import jax
import jax.numpy as jnp
from jax import lax
from jax.experimental import pallas as pl
from jax.experimental.pallas import tpu as pltpu
from jax.sharding import PartitionSpec as P

MESH = pl.DeviceIdType.MESH
F32 = jnp.float32
BF16 = jnp.bfloat16
NT = (((1,), (1,)), ((), ()))
NN = (((1,), (0,)), ((), ()))
dead_offset = 1e37


def dot(a, b, dims=NN):
    return lax.dot_general(a, b, dims, preferred_element_type=F32)


def swap_sets(rows):
    half = rows.shape[0] // 2
    return jnp.concatenate((rows[half:], rows[:half]), 0)


def kernel(
    n_dp,
    counts,
    lengths,
    owners,
    gate,
    q_hbm,
    g_hbm,
    k_hbm,
    v_hbm,
    dq_out,
    dk_out,
    dv_out,
    slot_tile,
    qbuf,
    graw,
    gt,
    kbuf,
    vbuf,
    kt,
    vt,
    pbuf,
    sbuf,
    stat_own,
    stat_got,
    cbuf,
    d_own,
    d_got,
    dbuf,
    dvs,
    dks,
    dq_give,
    dq_own,
    dq_got,
    dq_stage,
    k_send,
    k_recv,
    v_send,
    v_recv,
    dv_send,
    dv_recv,
    dk_send,
    dk_recv,
    q_send,
    q_recv,
    g_send,
    g_recv,
    st_send,
    st_recv,
    d_send,
    d_recv,
    dq_send,
    dq_recv,
    local,
    out_sem,
):
    samples, text, _ = q_hbm.shape
    half_tile, head_dim = kbuf.shape[1:]
    heads = q_hbm.shape[2] // head_dim
    both = 2 * heads
    tiles = owners.shape[1]
    set_rows = heads * text
    scale = head_dim ** (-0.5)
    to_log2 = scale * math.log2(math.e)

    me = lax.axis_index("dp")
    side = lax.axis_index("tensor")
    mate = side + 1 - 2 * (side % 2)

    def peer(i):
        return (me + (2 * (i % 2) - 1) * ((i + 1) // 2) + n_dp) % n_dp

    def to_dp(src, dst, send, recv, other):
        return pltpu.make_async_remote_copy(
            src, dst, send, recv, device_id={"dp": other}, device_id_type=MESH
        )

    def to_mate(src, dst, send, recv):
        return pltpu.make_async_remote_copy(
            src, dst, send, recv, device_id={"tensor": mate}, device_id_type=MESH
        )

    def k_copy(other):
        return to_dp(k_hbm.at[other], kbuf.at[me], k_send.at[other], k_recv.at[me], other)

    def v_copy(other):
        return to_dp(v_hbm.at[other], vbuf.at[me], v_send.at[other], v_recv.at[me], other)

    def dv_copy(other):
        return to_dp(dvs.at[other], dv_out.at[me], dv_send.at[other], dv_recv.at[me], other)

    def dk_copy(other):
        return to_dp(dks.at[other], dk_out.at[me], dk_send.at[other], dk_recv.at[me], other)

    def landed(buf, recv, other):
        to_dp(buf.at[other], buf.at[other], recv.at[other], recv.at[other], other).wait_recv()

    def head_cols(ref, h):
        return ref.at[:, :, pl.ds(h * head_dim, head_dim)]

    def head_rows(ref, hh):
        return ref.at[:, pl.ds(hh * text, text), :]

    def q_copy(h):
        return to_mate(
            head_cols(q_hbm, h), head_rows(qbuf, heads + h), q_send.at[h], q_recv.at[h]
        )

    def g_copy(h):
        return to_mate(
            head_cols(g_hbm, h), head_rows(graw, heads + h), g_send.at[h], g_recv.at[h]
        )

    def stat_copy(b):
        return to_mate(stat_own.at[b], stat_got.at[b], st_send.at[b], st_recv.at[b])

    def d_copy(b):
        return to_mate(d_own.at[b], d_got.at[b], d_send.at[b], d_recv.at[b])

    def dq_copy(b):
        return to_mate(dq_give.at[b], dq_got.at[b], dq_send.at[b], dq_recv.at[b])

    barrier = pltpu.get_barrier_semaphore()

    def greet(i, _):
        pl.semaphore_signal(
            barrier, inc=1, device_id={"dp": peer(i)}, device_id_type=MESH
        )
        return 0

    lax.fori_loop(1, n_dp, greet, 0)
    pl.semaphore_signal(barrier, inc=1, device_id={"tensor": mate}, device_id_type=MESH)
    pl.semaphore_wait(barrier, n_dp)

    def start_k(i, _):
        k_copy(peer(i)).start()
        return 0

    lax.fori_loop(1, n_dp, start_k, 0)
    for h in range(heads):
        q_copy(h).start()
    here = [
        pltpu.make_async_copy(k_hbm.at[me], kbuf.at[me], local.at[0]),
        pltpu.make_async_copy(v_hbm.at[me], vbuf.at[me], local.at[1]),
    ]
    for h in range(heads):
        here.append(
            pltpu.make_async_copy(head_cols(q_hbm, h), head_rows(qbuf, h), local.at[2 + 2 * h])
        )
        here.append(
            pltpu.make_async_copy(head_cols(g_hbm, h), head_rows(graw, h), local.at[3 + 2 * h])
        )
    for copy in here:
        copy.start()

    def find_tile(o, _):
        tile = jnp.int32(0)
        for b in range(samples):
            for j in range(tiles):
                tile = jnp.where(owners[b, j] == o, b * tiles + j, tile)
        slot_tile[o] = tile
        return 0

    lax.fori_loop(0, n_dp, find_tile, 0)
    for copy in here:
        copy.wait()

    def next_v(i, _):
        k_copy(peer(i)).wait_send()
        v_copy(peer(i)).start()
        return 0

    step = (n_dp + heads - 1) // heads
    for h in range(heads):
        lax.fori_loop(max(1, h * step), min(n_dp, (h + 1) * step), next_v, 0)
        q_copy(h).wait_send()
        g_copy(h).start()

    def wait_k(i, _):
        landed(kbuf, k_recv, peer(i))
        return 0

    lax.fori_loop(1, n_dp, wait_k, 0)
    for h in range(heads):
        q_copy(h).wait_recv()

    chunk = 32

    def weigh(b):
        def one_head(hh, _):
            row = pl.multiple_of(hh * text, text)
            q = qbuf[b, pl.ds(row, text), :]
            count = counts[b]
            top = None
            for j in range(tiles):
                s = dot(kbuf[owners[b, j]], q, NT)
                sbuf[j] = s
                tile_top = jnp.max(s, axis=0, keepdims=True)
                top = (
                    tile_top
                    if top is None
                    else jnp.maximum(top, jnp.where(j < count, tile_top, -1e37))
                )
            top = top * to_log2
            total = jnp.zeros((8, text), F32)
            for j in range(tiles):
                off = jnp.where(j < count, top, dead_offset)
                for r in range(half_tile // chunk):
                    x = sbuf[j, r * chunk : (r + 1) * chunk, :]
                    p = jnp.exp2(x * to_log2 - off)
                    total = total + jnp.sum(p.reshape(chunk // 8, 8, text), axis=0)
                    pbuf[b * tiles + j, r * chunk : (r + 1) * chunk, pl.ds(row, text)] = (
                        p.astype(BF16)
                    )
            stat_own[b, 0, pl.ds(hh, 1), :] = top
            stat_own[b, 1, pl.ds(hh, 1), :] = jnp.sum(total, axis=0, keepdims=True)
            return 0

        lax.fori_loop(0, both, one_head, 0)

    def weigh_sample(b, _):
        weigh(b)
        stat_copy(b).start()
        return 0

    lax.fori_loop(0, samples, weigh_sample, 0)

    gain = jnp.tanh(jnp.full((1, text), gate[0], F32))

    def join_stats(b, _):
        stat_copy(b).wait()
        top, total = stat_own[b, 0], stat_own[b, 1]
        top_got, total_got = swap_sets(stat_got[b, 0]), swap_sets(stat_got[b, 1])
        peak = jnp.maximum(top, top_got)
        mine = jnp.exp2(top - peak)
        cbuf[b] = mine / (total * mine + total_got * jnp.exp2(top_got - peak))
        return 0

    lax.fori_loop(0, samples, join_stats, 0)

    def scale_grad(first):
        def one(it, _):
            b = it // heads
            hh = first + it % heads
            row = pl.multiple_of(hh * text, text)
            x = graw[b, pl.ds(row, text), :].astype(F32).T
            live = lax.broadcasted_iota(jnp.int32, x.shape, 1) < lengths[b]
            x = jnp.where(live, x * gain, 0.0).astype(BF16).astype(F32)
            gt[b, :, pl.ds(row, text)] = (x * cbuf[b, pl.ds(hh, 1), :]).astype(BF16)
            return 0

        lax.fori_loop(0, samples * heads, one, 0)

    scale_grad(0)
    for h in range(heads):
        g_copy(h).wait_recv()
    scale_grad(heads)

    def value_tile(o):
        tile = slot_tile[o]
        b = tile // tiles
        total = jnp.zeros((half_tile, head_dim), F32)
        for hh in range(both):
            cols = slice(hh * text, (hh + 1) * text)
            total = total + dot(pbuf[tile, :, cols], gt[b, :, cols], NT)
        dvs[o] = total.astype(BF16)

    def key_tile(o):
        tile = slot_tile[o]
        b = tile // tiles
        total = jnp.zeros((half_tile, head_dim), F32)
        for hh in range(both):
            cols = slice(hh * text, (hh + 1) * text)
            total = total + dot(pbuf[tile, :, cols], qbuf[b, cols, :])
        dks[o] = (total * scale).astype(BF16)

    def give_value(i, _):
        value_tile(peer(i))
        dv_copy(peer(i)).start()
        return 0

    lax.fori_loop(1, n_dp, give_value, 0)
    value_tile(me)
    dv_keep = pltpu.make_async_copy(dvs.at[me], dv_out.at[me], out_sem.at[0])
    dv_keep.start()

    def wait_v(i, _):
        landed(vbuf, v_recv, peer(i))
        return 0

    lax.fori_loop(1, n_dp, wait_v, 0)

    def turn(it, _):
        b, j = it // tiles, it % tiles
        own = owners[b, j]
        kt[it] = kbuf[own].astype(F32).T.astype(BF16)
        vt[it] = vbuf[own].astype(F32).T.astype(BF16)
        return 0

    lax.fori_loop(0, samples * tiles, turn, 0)

    def delta_sample(b, _):
        def one_head(hh, _):
            row = pl.multiple_of(hh * text, text)
            total = jnp.zeros((head_dim, text), F32)
            for j in range(tiles):
                total = total + dot(vt[b * tiles + j], pbuf[b * tiles + j, :, pl.ds(row, text)])
            d_own[b, pl.ds(hh, 1), :] = jnp.sum(
                total * gt[b, :, pl.ds(row, text)].astype(F32), axis=0, keepdims=True
            )
            return 0

        lax.fori_loop(0, both, one_head, 0)
        d_copy(b).start()
        return 0

    lax.fori_loop(0, samples, delta_sample, 0)

    def score_sample(b, _):
        d_copy(b).wait()
        dbuf[...] = cbuf[b] * (d_own[b] + swap_sets(d_got[b]))

        def one_head(hh):
            row = pl.multiple_of(hh * text, text)
            g = gt[b, :, pl.ds(row, text)]
            delta = dbuf[pl.ds(hh, 1), :]
            total = jnp.zeros((head_dim, text), F32)
            for j in range(tiles):
                at = b * tiles + j
                gw = dot(vbuf[owners[b, j]], g)
                ds = (pbuf[at, :, pl.ds(row, text)].astype(F32) * (gw - delta)).astype(BF16)
                pbuf[at, :, pl.ds(row, text)] = ds
                total = total + dot(kt[at], ds)
            return (total * scale).T

        def give_head(h, _):
            dq_give[b, h] = one_head(heads + h).astype(BF16)
            return 0

        def keep_head(h, _):
            dq_own[b, h] = one_head(h)
            return 0

        lax.fori_loop(0, heads, give_head, 0)
        dq_copy(b).start()
        lax.fori_loop(0, heads, keep_head, 0)
        return 0

    lax.fori_loop(0, samples, score_sample, 0)

    def give_key(i, _):
        key_tile(peer(i))
        dk_copy(peer(i)).start()
        return 0

    lax.fori_loop(1, n_dp, give_key, 0)
    key_tile(me)
    dk_keep = pltpu.make_async_copy(dks.at[me], dk_out.at[me], out_sem.at[1])
    dk_keep.start()

    def join_queries(b, _):
        dq_copy(b).wait()
        for h in range(heads):
            dq_stage[b, :, h * head_dim : (h + 1) * head_dim] = (
                dq_own[b, h] + dq_got[b, h].astype(F32)
            ).astype(BF16)
        return 0

    lax.fori_loop(0, samples, join_queries, 0)
    dq_keep = pltpu.make_async_copy(dq_stage, dq_out, out_sem.at[2])
    dq_keep.start()

    for h in range(heads):
        g_copy(h).wait_send()

    def finish(i, _):
        other = peer(i)
        v_copy(other).wait_send()
        dv_copy(other).wait_send()
        dk_copy(other).wait_send()
        landed(dv_out, dv_recv, other)
        landed(dk_out, dk_recv, other)
        return 0

    lax.fori_loop(1, n_dp, finish, 0)
    dv_keep.wait()
    dk_keep.wait()
    dq_keep.wait()


def shards(
    n_dp,
    queries,
    grad_output,
    image_keys,
    image_values,
    attn_gate,
    image_counts,
    text_lengths,
    tile_owner,
):
    samples, text, width = queries.shape
    _, slots, half_tile, head_dim = image_keys.shape
    heads = width // head_dim
    both = 2 * heads
    tiles = tile_owner.shape[1]
    rows = both * text
    stored = (slots, half_tile, head_dim)
    smem = pl.BlockSpec(memory_space=pltpu.SMEM)
    hbm = pl.BlockSpec(memory_space=pl.ANY)
    dma = pltpu.SemaphoreType.DMA
    dq, dk, dv = pl.pallas_call(
        functools.partial(kernel, n_dp),
        out_shape=(
            jax.ShapeDtypeStruct(queries.shape, BF16),
            jax.ShapeDtypeStruct(stored, BF16),
            jax.ShapeDtypeStruct(stored, BF16),
        ),
        in_specs=[smem] * 4 + [hbm] * 4,
        out_specs=(hbm, hbm, hbm),
        scratch_shapes=[
            pltpu.SMEM((slots,), jnp.int32),
            pltpu.VMEM((samples, rows, head_dim), BF16),
            pltpu.VMEM((samples, rows, head_dim), BF16),
            pltpu.VMEM((samples, head_dim, rows), BF16),
            pltpu.VMEM(stored, BF16),
            pltpu.VMEM(stored, BF16),
            pltpu.VMEM((slots, head_dim, half_tile), BF16),
            pltpu.VMEM((slots, head_dim, half_tile), BF16),
            pltpu.VMEM((slots, half_tile, rows), BF16),
            pltpu.VMEM((tiles, half_tile, text), F32),
            pltpu.VMEM((samples, 2, both, text), F32),
            pltpu.VMEM((samples, 2, both, text), F32),
            pltpu.VMEM((samples, both, text), F32),
            pltpu.VMEM((samples, both, text), F32),
            pltpu.VMEM((samples, both, text), F32),
            pltpu.VMEM((both, text), F32),
            pltpu.VMEM(stored, BF16),
            pltpu.VMEM(stored, BF16),
            pltpu.VMEM((samples, heads, text, head_dim), BF16),
            pltpu.VMEM((samples, heads, text, head_dim), F32),
            pltpu.VMEM((samples, heads, text, head_dim), BF16),
            pltpu.VMEM((samples, text, width), BF16),
        ]
        + [dma((slots,))] * 8
        + [dma((heads,))] * 4
        + [dma((samples,))] * 6
        + [dma((2 + 2 * heads,)), dma((3,))],
        compiler_params=pltpu.CompilerParams(
            collective_id=0, has_side_effects=True, vmem_limit_bytes=56 * 2**20
        ),
        name="cross_attention_backward",
    )(
        image_counts,
        text_lengths,
        tile_owner,
        attn_gate,
        queries,
        grad_output,
        image_keys[0],
        image_values[0],
    )
    return dq, dk[None], dv[None]


def solution(mesh):
    return jax.shard_map(
        functools.partial(shards, mesh.shape["dp"]),
        mesh=mesh,
        in_specs=(
            P("dp", None, "tensor"),
            P("dp", None, "tensor"),
            P("tensor", "dp", None, None),
            P("tensor", "dp", None, None),
            P(),
            P("dp"),
            P("dp"),
            P("dp", None),
        ),
        out_specs=(
            P("dp", None, "tensor"),
            P("tensor", "dp", None, None),
            P("tensor", "dp", None, None),
        ),
        check_vma=False,
    )
```

time: 333 us -> 131 us (0.39); the launches traced: 329 us -> 131 us
  waiting for transfers between devices: 153 us -> 0 us
  Pallas kernels: 0 us -> 125 us
  matrix products: 67.1 us -> 0 us
  blocking collectives: 34.2 us -> 0 us
  local copies, waits for them, and re-layouts: 30.8 us -> 4.93 us
  starting transfers between devices: 25 us -> 0 us
  other arithmetic: 17.7 us -> 0 us
    pallas_call x0 -> x1, Pallas kernels: none -> 125 us  [shards(): pl.pallas_call(functools.partial(kernel, n_dp), out_shape=(jax.ShapeDtype...]
    all_to_all x3 -> x0, waiting for transfers between devices: 112 us -> none  [the longest x1 45.8 us: shards(): lax.all_to_all(value_owned, 'dp', split_axis=0, concat_axis=0, tiled=True)]
    dot_general x16 -> x0, matrix products: 43.2 us -> none  [the longest x4 22.4 us: per_sample(): jnp.einsum('htk,thd->kd', weights_low, grad_heads, preferred_element_type...]
    ppermute x4 -> x0, waiting for transfers between devices: 40.6 us -> none  [swapped(): return lax.ppermute(block, axis, route)]
    all_to_all x1 -> x0, blocking collectives: 34.2 us -> none  [shards(): lax.all_to_all(image_values, 'dp', split_axis=1, concat_axis=1, tiled=True)]
    sub x4 -> x0, matrix products: 23.9 us -> none  [per_sample(): exponent = jnp.exp(scores - row_top)]
    all_to_all x3 -> x0, starting transfers between devices: 19 us -> none  [the longest x1 6.55 us: shards(): lax.all_to_all(value_owned, 'dp', split_axis=0, concat_axis=0, tiled=True)]
    gather x4 -> x0, local copies, waits for them, and re-layouts: 14 us -> none  [the longest x1 3.88 us: shards(): key_parts.reshape(sample_count * tile_slots, tile_rows, head_dim)]
  transfers between devices with their start and end apart: 7 -> 0, of which waited for: 5 -> 0; matrix products, arithmetic and copies ran while one was open for 4% -> 0% of each run, Pallas kernels for 0% -> 0%
where the time goes in v1:
time: 131 us
  Pallas kernels  125 us (95%)
  local copies, waits for them, and re-layouts  4.93 us (4%)
    pallas_call x1, Pallas kernels, shards(): pl.pallas_call(functools.partial(kernel, n_dp), out_shape=(jax.ShapeDtype...  125 us
    unnamed x7, local copies, waits for them, and re-layouts  4.93 us

profile of v1, /device:TPU:40, one launch (start us, length us, event | category | flops | bytes accessed | tf_op | source)
XLA Modules:
  0.0 130.9 jit_solution(13823561097526804382)
XLA Ops:
  1.3 124.7 %cross_attention_backward.1 = (bf16[4,256,512]{2,1,0:T(8,128)(2,1)}, bf16[16,256,128]{2,1,0:T(8,128)(2,1)}, bf16[16,256,128]{2,1,0:T(8,128)(2,1)}) custom-call(s32[4]{0:T(128)} %counts.1, s32[4]{0:T(128)} %lengths.1, s32[4,4]{1,0:T(4,128)} %owners.1, f32[1]{0:T(128)S(6)} %copy.14.gate, bf16[4,256,512]{2,1,0:T(8,128)(2,1)} %q_hbm.1, ...), custom_call_target="tpu_custom_call" | custom-call | tf_op jit(solution)/shard_map/cross_attention_backward/pallas_call | solution.py:439
  125.9 0.0 copy-start.1
  125.9 2.4 %copy.15 = bf16[4,256,512]{2,1,0:T(8,128)(2,1)} copy(bf16[4,256,512]{2,1,0:T(8,128)(2,1)} %get-tuple-element.12) | data formatting | bytes 2097152
  128.3 0.0 copy-done.1
  128.3 0.0 copy-start
  128.3 1.0 copy.16
  129.3 0.6 copy-done
  129.9 1.0 copy.17
Async XLA Ops:
  125.9 2.4 %copy-start.1 = (bf16[16,256,128]{2,1,0:T(8,128)(2,1)S(1)}, bf16[16,256,128]{2,1,0:T(8,128)(2,1)}, u32[]{:S(2)}) copy-start(bf16[16,256,128]{2,1,0:T(8,128)(2,1)} %get-tuple-element.7) | copy-start | bytes 3145732
  128.3 1.6 %copy-start = (bf16[16,256,128]{2,1,0:T(8,128)(2,1)S(1)}, bf16[16,256,128]{2,1,0:T(8,128)(2,1)}, u32[]{:S(2)}) copy-start(bf16[16,256,128]{2,1,0:T(8,128)(2,1)} %get-tuple-element.8) | copy-start | bytes 3145732

commit v2 on v1

--- a/solution.py
+++ b/solution.py
@@ -14,6 +14,7 @@
 NT = (((1,), (1,)), ((), ()))
 NN = (((1,), (0,)), ((), ()))
 dead_offset = 1e37
+group_size = 2
 
 
 def dot(a, b, dims=NN):
@@ -54,6 +55,7 @@
     d_own,
     d_got,
     dbuf,
+    dv_part,
     dvs,
     dks,
     dq_give,
@@ -95,7 +97,8 @@
     mate = side + 1 - 2 * (side % 2)
 
     def peer(i):
-        return (me + (2 * (i % 2) - 1) * ((i + 1) // 2) + n_dp) % n_dp
+        near = n_dp - i
+        return (me + (2 * (near % 2) - 1) * ((near + 1) // 2) + n_dp) % n_dp
 
     def to_dp(src, dst, send, recv, other):
         return pltpu.make_async_remote_copy(
@@ -122,21 +125,11 @@
     def landed(buf, recv, other):
         to_dp(buf.at[other], buf.at[other], recv.at[other], recv.at[other], other).wait_recv()
 
-    def head_cols(ref, h):
-        return ref.at[:, :, pl.ds(h * head_dim, head_dim)]
-
-    def head_rows(ref, hh):
-        return ref.at[:, pl.ds(hh * text, text), :]
-
-    def q_copy(h):
-        return to_mate(
-            head_cols(q_hbm, h), head_rows(qbuf, heads + h), q_send.at[h], q_recv.at[h]
-        )
-
-    def g_copy(h):
-        return to_mate(
-            head_cols(g_hbm, h), head_rows(graw, heads + h), g_send.at[h], g_recv.at[h]
-        )
+    def q_copy(b):
+        return to_mate(q_hbm.at[b], qbuf.at[1, b], q_send.at[b], q_recv.at[b])
+
+    def g_copy(b):
+        return to_mate(g_hbm.at[b], graw.at[1, b], g_send.at[b], g_recv.at[b])
 
     def stat_copy(b):
         return to_mate(stat_own.at[b], stat_got.at[b], st_send.at[b], st_recv.at[b])
@@ -164,19 +157,14 @@
         return 0
 
     lax.fori_loop(1, n_dp, start_k, 0)
-    for h in range(heads):
-        q_copy(h).start()
+    for b in range(samples):
+        q_copy(b).start()
     here = [
         pltpu.make_async_copy(k_hbm.at[me], kbuf.at[me], local.at[0]),
         pltpu.make_async_copy(v_hbm.at[me], vbuf.at[me], local.at[1]),
+        pltpu.make_async_copy(q_hbm, qbuf.at[0], local.at[2]),
+        pltpu.make_async_copy(g_hbm, graw.at[0], local.at[3]),
     ]
-    for h in range(heads):
-        here.append(
-            pltpu.make_async_copy(head_cols(q_hbm, h), head_rows(qbuf, h), local.at[2 + 2 * h])
-        )
-        here.append(
-            pltpu.make_async_copy(head_cols(g_hbm, h), head_rows(graw, h), local.at[3 + 2 * h])
-        )
     for copy in here:
         copy.start()
 
@@ -192,58 +180,69 @@
     for copy in here:
         copy.wait()
 
-    def next_v(i, _):
+    def sent_k(i, _):
         k_copy(peer(i)).wait_send()
+        return 0
+
+    def start_v(i, _):
         v_copy(peer(i)).start()
         return 0
 
-    step = (n_dp + heads - 1) // heads
-    for h in range(heads):
-        lax.fori_loop(max(1, h * step), min(n_dp, (h + 1) * step), next_v, 0)
-        q_copy(h).wait_send()
-        g_copy(h).start()
+    for b in range(samples):
+        q_copy(b).wait_send()
+        g_copy(b).start()
+    lax.fori_loop(1, n_dp, sent_k, 0)
+    lax.fori_loop(1, n_dp, start_v, 0)
 
     def wait_k(i, _):
         landed(kbuf, k_recv, peer(i))
         return 0
 
     lax.fori_loop(1, n_dp, wait_k, 0)
-    for h in range(heads):
-        q_copy(h).wait_recv()
+    for b in range(samples):
+        q_copy(b).wait_recv()
 
     chunk = 32
 
+    def cols_of(h):
+        return slice(h * head_dim, (h + 1) * head_dim)
+
+    def rows_of(hh):
+        return slice(hh * text, (hh + 1) * text)
+
     def weigh(b):
-        def one_head(hh, _):
-            row = pl.multiple_of(hh * text, text)
-            q = qbuf[b, pl.ds(row, text), :]
+        def one_set(which, _):
             count = counts[b]
-            top = None
-            for j in range(tiles):
-                s = dot(kbuf[owners[b, j]], q, NT)
-                sbuf[j] = s
-                tile_top = jnp.max(s, axis=0, keepdims=True)
-                top = (
-                    tile_top
-                    if top is None
-                    else jnp.maximum(top, jnp.where(j < count, tile_top, -1e37))
-                )
-            top = top * to_log2
-            total = jnp.zeros((8, text), F32)
-            for j in range(tiles):
-                off = jnp.where(j < count, top, dead_offset)
-                for r in range(half_tile // chunk):
-                    x = sbuf[j, r * chunk : (r + 1) * chunk, :]
-                    p = jnp.exp2(x * to_log2 - off)
-                    total = total + jnp.sum(p.reshape(chunk // 8, 8, text), axis=0)
-                    pbuf[b * tiles + j, r * chunk : (r + 1) * chunk, pl.ds(row, text)] = (
-                        p.astype(BF16)
+            for h in range(heads):
+                hh = which * heads + h
+                row = pl.multiple_of(hh * text, text)
+                q = qbuf[which, b, :, cols_of(h)]
+                top = None
+                for j in range(tiles):
+                    s = dot(kbuf[owners[b, j]], q, NT)
+                    sbuf[h, j] = s
+                    tile_top = jnp.max(s, axis=0, keepdims=True)
+                    top = (
+                        tile_top
+                        if top is None
+                        else jnp.maximum(top, jnp.where(j < count, tile_top, -1e37))
                     )
-            stat_own[b, 0, pl.ds(hh, 1), :] = top
-            stat_own[b, 1, pl.ds(hh, 1), :] = jnp.sum(total, axis=0, keepdims=True)
+                top = top * to_log2
+                total = jnp.zeros((8, text), F32)
+                for j in range(tiles):
+                    off = jnp.where(j < count, top, dead_offset)
+                    for r in range(half_tile // chunk):
+                        x = sbuf[h, j, r * chunk : (r + 1) * chunk, :]
+                        p = jnp.exp2(x * to_log2 - off)
+                        total = total + jnp.sum(p.reshape(chunk // 8, 8, text), axis=0)
+                        pbuf[b * tiles + j, r * chunk : (r + 1) * chunk, pl.ds(row, text)] = (
+                            p.astype(BF16)
+                        )
+                stat_own[b, 0, pl.ds(hh, 1), :] = top
+                stat_own[b, 1, pl.ds(hh, 1), :] = jnp.sum(total, axis=0, keepdims=True)
             return 0
 
-        lax.fori_loop(0, both, one_head, 0)
+        lax.fori_loop(0, 2, one_set, 0)
 
     def weigh_sample(b, _):
         weigh(b)
@@ -265,48 +264,70 @@
 
     lax.fori_loop(0, samples, join_stats, 0)
 
-    def scale_grad(first):
-        def one(it, _):
-            b = it // heads
-            hh = first + it % heads
-            row = pl.multiple_of(hh * text, text)
-            x = graw[b, pl.ds(row, text), :].astype(F32).T
-            live = lax.broadcasted_iota(jnp.int32, x.shape, 1) < lengths[b]
+    def scale_grad(which, b):
+        live = lax.broadcasted_iota(jnp.int32, (head_dim, text), 1) < lengths[b]
+        for h in range(heads):
+            hh = which * heads + h
+            x = graw[which, b, :, cols_of(h)].astype(F32).T
             x = jnp.where(live, x * gain, 0.0).astype(BF16).astype(F32)
-            gt[b, :, pl.ds(row, text)] = (x * cbuf[b, pl.ds(hh, 1), :]).astype(BF16)
-            return 0
-
-        lax.fori_loop(0, samples * heads, one, 0)
-
-    scale_grad(0)
-    for h in range(heads):
-        g_copy(h).wait_recv()
-    scale_grad(heads)
-
-    def value_tile(o):
+            gt[b, :, rows_of(hh)] = (x * cbuf[b, hh : hh + 1, :]).astype(BF16)
+
+    def value_sum(o, first):
         tile = slot_tile[o]
         b = tile // tiles
         total = jnp.zeros((half_tile, head_dim), F32)
-        for hh in range(both):
-            cols = slice(hh * text, (hh + 1) * text)
-            total = total + dot(pbuf[tile, :, cols], gt[b, :, cols], NT)
-        dvs[o] = total.astype(BF16)
+        for hh in range(first, first + heads):
+            total = total + dot(pbuf[tile, :, rows_of(hh)], gt[b, :, rows_of(hh)], NT)
+        return total
+
+    def scale_own(b, _):
+        scale_grad(0, b)
+        return 0
+
+    lax.fori_loop(0, samples, scale_own, 0)
+
+    def start_value(o, _):
+        dv_part[o] = value_sum(o, 0)
+        return 0
+
+    lax.fori_loop(0, n_dp, start_value, 0, unroll=4)
+
+    def turn_keys(it, _):
+        kt[it] = kbuf[owners[it // tiles, it % tiles]].astype(F32).T.astype(BF16)
+        return 0
+
+    lax.fori_loop(0, samples * tiles, turn_keys, 0, unroll=4)
+    def scale_got(b, _):
+        g_copy(b).wait_recv()
+        scale_grad(1, b)
+        return 0
+
+    lax.fori_loop(0, samples, scale_got, 0)
+
+    def value_tile(o):
+        dvs[o] = (dv_part[o] + value_sum(o, heads)).astype(BF16)
 
     def key_tile(o):
         tile = slot_tile[o]
         b = tile // tiles
         total = jnp.zeros((half_tile, head_dim), F32)
         for hh in range(both):
-            cols = slice(hh * text, (hh + 1) * text)
-            total = total + dot(pbuf[tile, :, cols], qbuf[b, cols, :])
+            total = total + dot(
+                pbuf[tile, :, rows_of(hh)], qbuf[hh // heads, b, :, cols_of(hh % heads)]
+            )
         dks[o] = (total * scale).astype(BF16)
 
-    def give_value(i, _):
-        value_tile(peer(i))
-        dv_copy(peer(i)).start()
-        return 0
-
-    lax.fori_loop(1, n_dp, give_value, 0)
+    def give_values(i, _):
+        group = [peer(group_size * i + 2 + k) for k in range(group_size)]
+        for other in group:
+            value_tile(other)
+        for other in group:
+            dv_copy(other).start()
+        return 0
+
+    value_tile(peer(1))
+    dv_copy(peer(1)).start()
+    lax.fori_loop(0, (n_dp - 2) // group_size, give_values, 0)
     value_tile(me)
     dv_keep = pltpu.make_async_copy(dvs.at[me], dv_out.at[me], out_sem.at[0])
     dv_keep.start()
@@ -317,14 +338,11 @@
 
     lax.fori_loop(1, n_dp, wait_v, 0)
 
-    def turn(it, _):
-        b, j = it // tiles, it % tiles
-        own = owners[b, j]
-        kt[it] = kbuf[own].astype(F32).T.astype(BF16)
-        vt[it] = vbuf[own].astype(F32).T.astype(BF16)
-        return 0
-
-    lax.fori_loop(0, samples * tiles, turn, 0)
+    def turn_values(it, _):
+        vt[it] = vbuf[owners[it // tiles, it % tiles]].astype(F32).T.astype(BF16)
+        return 0
+
+    lax.fori_loop(0, samples * tiles, turn_values, 0, unroll=4)
 
     def delta_sample(b, _):
         def one_head(hh, _):
@@ -337,7 +355,7 @@
             )
             return 0
 
-        lax.fori_loop(0, both, one_head, 0)
+        lax.fori_loop(0, both, one_head, 0, unroll=4)
         d_copy(b).start()
         return 0
 
@@ -368,19 +386,24 @@
             dq_own[b, h] = one_head(h)
             return 0
 
-        lax.fori_loop(0, heads, give_head, 0)
+        lax.fori_loop(0, heads, give_head, 0, unroll=4)
         dq_copy(b).start()
-        lax.fori_loop(0, heads, keep_head, 0)
+        lax.fori_loop(0, heads, keep_head, 0, unroll=4)
         return 0
 
     lax.fori_loop(0, samples, score_sample, 0)
 
-    def give_key(i, _):
-        key_tile(peer(i))
-        dk_copy(peer(i)).start()
-        return 0
-
-    lax.fori_loop(1, n_dp, give_key, 0)
+    def give_keys(i, _):
+        group = [peer(group_size * i + 2 + k) for k in range(group_size)]
+        for other in group:
+            key_tile(other)
+        for other in group:
+            dk_copy(other).start()
+        return 0
+
+    key_tile(peer(1))
+    dk_copy(peer(1)).start()
+    lax.fori_loop(0, (n_dp - 2) // group_size, give_keys, 0)
     key_tile(me)
     dk_keep = pltpu.make_async_copy(dks.at[me], dk_out.at[me], out_sem.at[1])
     dk_keep.start()
@@ -397,8 +420,8 @@
     dq_keep = pltpu.make_async_copy(dq_stage, dq_out, out_sem.at[2])
     dq_keep.start()
 
-    for h in range(heads):
-        g_copy(h).wait_send()
+    for b in range(samples):
+        g_copy(b).wait_send()
 
     def finish(i, _):
         other = peer(i)
@@ -413,6 +436,27 @@
     dv_keep.wait()
     dk_keep.wait()
     dq_keep.wait()
+
+
+def place(dq, dk, dv, dq_out, dk_out, dv_out, dq_buf, dk_buf, dv_buf, get_sem, put_sem):
+    moves = []
+    for src, buf, dst in ((dq, dq_buf, dq_out), (dk, dk_buf, dk_out), (dv, dv_buf, dv_out)):
+        half = src.shape[0] // 2
+        for part in (pl.ds(0, half), pl.ds(half, half)):
+            at = len(moves)
+            moves.append(
+                (
+                    pltpu.make_async_copy(src.at[part], buf.at[part], get_sem.at[at]),
+                    pltpu.make_async_copy(buf.at[part], dst.at[part], put_sem.at[at]),
+                )
+            )
+    for get, _ in moves:
+        get.start()
+    for get, put in moves:
+        get.wait()
+        put.start()
+    for _, put in moves:
+        put.wait()
 
 
 def shards(
@@ -436,32 +480,34 @@
     smem = pl.BlockSpec(memory_space=pltpu.SMEM)
     hbm = pl.BlockSpec(memory_space=pl.ANY)
     dma = pltpu.SemaphoreType.DMA
-    dq, dk, dv = pl.pallas_call(
+    results = (
+        jax.ShapeDtypeStruct(queries.shape, BF16),
+        jax.ShapeDtypeStruct(stored, BF16),
+        jax.ShapeDtypeStruct(stored, BF16),
+    )
+    made = pl.pallas_call(
         functools.partial(kernel, n_dp),
-        out_shape=(
-            jax.ShapeDtypeStruct(queries.shape, BF16),
-            jax.ShapeDtypeStruct(stored, BF16),
-            jax.ShapeDtypeStruct(stored, BF16),
-        ),
+        out_shape=results,
         in_specs=[smem] * 4 + [hbm] * 4,
         out_specs=(hbm, hbm, hbm),
         scratch_shapes=[
             pltpu.SMEM((slots,), jnp.int32),
-            pltpu.VMEM((samples, rows, head_dim), BF16),
-            pltpu.VMEM((samples, rows, head_dim), BF16),
+            pltpu.VMEM((2,) + queries.shape, BF16),
+            pltpu.VMEM((2,) + queries.shape, BF16),
             pltpu.VMEM((samples, head_dim, rows), BF16),
             pltpu.VMEM(stored, BF16),
             pltpu.VMEM(stored, BF16),
             pltpu.VMEM((slots, head_dim, half_tile), BF16),
             pltpu.VMEM((slots, head_dim, half_tile), BF16),
             pltpu.VMEM((slots, half_tile, rows), BF16),
-            pltpu.VMEM((tiles, half_tile, text), F32),
+            pltpu.VMEM((heads, tiles, half_tile, text), F32),
             pltpu.VMEM((samples, 2, both, text), F32),
             pltpu.VMEM((samples, 2, both, text), F32),
             pltpu.VMEM((samples, both, text), F32),
             pltpu.VMEM((samples, both, text), F32),
             pltpu.VMEM((samples, both, text), F32),
             pltpu.VMEM((both, text), F32),
+            pltpu.VMEM(stored, F32),
             pltpu.VMEM(stored, BF16),
             pltpu.VMEM(stored, BF16),
             pltpu.VMEM((samples, heads, text, head_dim), BF16),
@@ -470,9 +516,8 @@
             pltpu.VMEM((samples, text, width), BF16),
         ]
         + [dma((slots,))] * 8
-        + [dma((heads,))] * 4
-        + [dma((samples,))] * 6
-        + [dma((2 + 2 * heads,)), dma((3,))],
+        + [dma((samples,))] * 10
+        + [dma((4,)), dma((3,))],
         compiler_params=pltpu.CompilerParams(
             collective_id=0, has_side_effects=True, vmem_limit_bytes=56 * 2**20
         ),
@@ -487,6 +532,14 @@
         image_keys[0],
         image_values[0],
     )
+    dq, dk, dv = pl.pallas_call(
+        place,
+        out_shape=results,
+        in_specs=[hbm] * 3,
+        out_specs=(hbm, hbm, hbm),
+        scratch_shapes=[pltpu.VMEM(leaf.shape, BF16) for leaf in results] + [dma((6,))] * 2,
+        name="place_results",
+    )(*made)
     return dq, dk[None], dv[None]
 
 

time: 131 us -> 116 us (0.89); the launches traced: 131 us -> 114 us
  Pallas kernels: 125 us -> 112 us
  local copies, waits for them, and re-layouts: 4.93 us -> 0 us
    pallas_call x1 -> x2, Pallas kernels: 125 us -> 112 us  [the longest x1 110 us: shards(): pl.pallas_call(functools.partial(kernel, n_dp), out_shape=results, in_spe...]
    unnamed x7 -> x0, local copies, waits for them, and re-layouts: 4.93 us -> none
where the time goes in v2:
time: 116 us; the launch traced here: 114 us
  Pallas kernels  112 us (97%)
  between operations  1.29 us (1%)
    pallas_call x1, Pallas kernels, shards(): pl.pallas_call(functools.partial(kernel, n_dp), out_shape=results, in_spe...  110 us
    pallas_call x1, Pallas kernels, shards(): pl.pallas_call(place, out_shape=results, in_specs=[hbm] * 3, out_specs=(h...  2.8 us

profile of v2, /device:TPU:40, one launch (start us, length us, event | category | flops | bytes accessed | tf_op | source)
XLA Modules:
  0.0 113.7 jit_solution(15118094421891915918)
XLA Ops:
  1.3 109.6 %cross_attention_backward.1 = (bf16[4,256,512]{2,1,0:T(8,128)(2,1)}, bf16[16,256,128]{2,1,0:T(8,128)(2,1)}, bf16[16,256,128]{2,1,0:T(8,128)(2,1)}) custom-call(s32[4]{0:T(128)} %counts.1, s32[4]{0:T(128)} %lengths.1, s32[4,4]{1,0:T(4,128)} %owners.1, f32[1]{0:T(128)S(6)} %copy.11.gate, bf16[4,256,512]{2,1,0:T(8,128)(2,1)} %q_hbm.1, ...), custom_call_target="tpu_custom_call" | custom-call | tf_op jit(solution)/shard_map/cross_attention_backward/pallas_call | solution.py:488
  110.9 2.8 %place_results.1 = (bf16[4,256,512]{2,1,0:T(8,128)(2,1)}, bf16[16,256,128]{2,1,0:T(8,128)(2,1)}, bf16[16,256,128]{2,1,0:T(8,128)(2,1)}) custom-call(bf16[4,256,512]{2,1,0:T(8,128)(2,1)} %get-tuple-element.9.dq, bf16[16,256,128]{2,1,0:T(8,128)(2,1)} %get-tuple-element.10.dk, bf16[16,256,128]{2,1,0:T(8,128)(2,1)} %get-tuple-element.11.dv), custom_call_target="tpu_custom_call" | custom-call | tf_op jit(solution)/shard_map/place_results/pallas_call | solution.py:535

commit v3 on v2

--- a/solution.py
+++ b/solution.py
@@ -14,6 +14,7 @@
 NT = (((1,), (1,)), ((), ()))
 NN = (((1,), (0,)), ((), ()))
 dead_offset = 1e37
+value_group = 2
 group_size = 2
 
 
@@ -80,7 +81,9 @@
     d_recv,
     dq_send,
     dq_recv,
-    local,
+    q_local,
+    g_local,
+    tile_local,
     out_sem,
 ):
     samples, text, _ = q_hbm.shape
@@ -88,7 +91,7 @@
     heads = q_hbm.shape[2] // head_dim
     both = 2 * heads
     tiles = owners.shape[1]
-    set_rows = heads * text
+    early = heads // 2
     scale = head_dim ** (-0.5)
     to_log2 = scale * math.log2(math.e)
 
@@ -128,8 +131,8 @@
     def q_copy(b):
         return to_mate(q_hbm.at[b], qbuf.at[1, b], q_send.at[b], q_recv.at[b])
 
-    def g_copy(b):
-        return to_mate(g_hbm.at[b], graw.at[1, b], g_send.at[b], g_recv.at[b])
+    def g_copy(h):
+        return to_mate(graw.at[0, h], graw.at[1, h], g_send.at[h], g_recv.at[h])
 
     def stat_copy(b):
         return to_mate(stat_own.at[b], stat_got.at[b], st_send.at[b], st_recv.at[b])
@@ -140,6 +143,19 @@
     def dq_copy(b):
         return to_mate(dq_give.at[b], dq_got.at[b], dq_send.at[b], dq_recv.at[b])
 
+    q_here = [
+        pltpu.make_async_copy(q_hbm.at[b], qbuf.at[0, b], q_local.at[b]) for b in range(samples)
+    ]
+    g_here = [
+        pltpu.make_async_copy(
+            g_hbm.at[:, :, pl.ds(h * head_dim, head_dim)], graw.at[0, h], g_local.at[h]
+        )
+        for h in range(heads)
+    ]
+    tile_here = [
+        pltpu.make_async_copy(k_hbm.at[me], kbuf.at[me], tile_local.at[0]),
+        pltpu.make_async_copy(v_hbm.at[me], vbuf.at[me], tile_local.at[1]),
+    ]
     barrier = pltpu.get_barrier_semaphore()
 
     def greet(i, _):
@@ -148,7 +164,7 @@
         )
         return 0
 
-    lax.fori_loop(1, n_dp, greet, 0)
+    lax.fori_loop(1, n_dp, greet, 0, unroll=True)
     pl.semaphore_signal(barrier, inc=1, device_id={"tensor": mate}, device_id_type=MESH)
     pl.semaphore_wait(barrier, n_dp)
 
@@ -156,16 +172,10 @@
         k_copy(peer(i)).start()
         return 0
 
-    lax.fori_loop(1, n_dp, start_k, 0)
+    lax.fori_loop(1, n_dp, start_k, 0, unroll=True)
     for b in range(samples):
         q_copy(b).start()
-    here = [
-        pltpu.make_async_copy(k_hbm.at[me], kbuf.at[me], local.at[0]),
-        pltpu.make_async_copy(v_hbm.at[me], vbuf.at[me], local.at[1]),
-        pltpu.make_async_copy(q_hbm, qbuf.at[0], local.at[2]),
-        pltpu.make_async_copy(g_hbm, graw.at[0], local.at[3]),
-    ]
-    for copy in here:
+    for copy in q_here + g_here + tile_here:
         copy.start()
 
     def find_tile(o, _):
@@ -177,7 +187,7 @@
         return 0
 
     lax.fori_loop(0, n_dp, find_tile, 0)
-    for copy in here:
+    for copy in q_here + g_here + tile_here:
         copy.wait()
 
     def sent_k(i, _):
@@ -190,9 +200,10 @@
 
     for b in range(samples):
         q_copy(b).wait_send()
-        g_copy(b).start()
+    for h in range(early):
+        g_copy(h).start()
     lax.fori_loop(1, n_dp, sent_k, 0)
-    lax.fori_loop(1, n_dp, start_v, 0)
+    lax.fori_loop(1, n_dp, start_v, 0, unroll=True)
 
     def wait_k(i, _):
         landed(kbuf, k_recv, peer(i))
@@ -249,7 +260,12 @@
         stat_copy(b).start()
         return 0
 
-    lax.fori_loop(0, samples, weigh_sample, 0)
+    lax.fori_loop(0, samples // 2, weigh_sample, 0)
+    for h in range(early):
+        g_copy(h).wait_send()
+    for h in range(early, heads):
+        g_copy(h).start()
+    lax.fori_loop(samples // 2, samples, weigh_sample, 0)
 
     gain = jnp.tanh(jnp.full((1, text), gate[0], F32))
 
@@ -264,48 +280,44 @@
 
     lax.fori_loop(0, samples, join_stats, 0)
 
-    def scale_grad(which, b):
-        live = lax.broadcasted_iota(jnp.int32, (head_dim, text), 1) < lengths[b]
-        for h in range(heads):
-            hh = which * heads + h
-            x = graw[which, b, :, cols_of(h)].astype(F32).T
+    def scale_grad(which, h):
+        rows = rows_of(which * heads + h)
+
+        def one(b, _):
+            x = graw[which, h, b].astype(F32).T
+            live = lax.broadcasted_iota(jnp.int32, x.shape, 1) < lengths[b]
             x = jnp.where(live, x * gain, 0.0).astype(BF16).astype(F32)
-            gt[b, :, rows_of(hh)] = (x * cbuf[b, hh : hh + 1, :]).astype(BF16)
-
-    def value_sum(o, first):
+            factor = cbuf[b, which * heads + h : which * heads + h + 1, :]
+            gt[b, :, rows] = (x * factor).astype(BF16)
+            return 0
+
+        lax.fori_loop(0, samples, one, 0, unroll=4)
+
+    def value_sum(o, first, number):
         tile = slot_tile[o]
         b = tile // tiles
         total = jnp.zeros((half_tile, head_dim), F32)
-        for hh in range(first, first + heads):
+        for hh in range(first, first + number):
             total = total + dot(pbuf[tile, :, rows_of(hh)], gt[b, :, rows_of(hh)], NT)
         return total
 
-    def scale_own(b, _):
-        scale_grad(0, b)
-        return 0
-
-    lax.fori_loop(0, samples, scale_own, 0)
+    for h in range(heads):
+        scale_grad(0, h)
+    for h in range(early):
+        g_copy(h).wait_recv()
+        scale_grad(1, h)
 
     def start_value(o, _):
-        dv_part[o] = value_sum(o, 0)
+        dv_part[o] = value_sum(o, 0, heads + early)
         return 0
 
     lax.fori_loop(0, n_dp, start_value, 0, unroll=4)
-
-    def turn_keys(it, _):
-        kt[it] = kbuf[owners[it // tiles, it % tiles]].astype(F32).T.astype(BF16)
-        return 0
-
-    lax.fori_loop(0, samples * tiles, turn_keys, 0, unroll=4)
-    def scale_got(b, _):
-        g_copy(b).wait_recv()
-        scale_grad(1, b)
-        return 0
-
-    lax.fori_loop(0, samples, scale_got, 0)
+    for h in range(early, heads):
+        g_copy(h).wait_recv()
+        scale_grad(1, h)
 
     def value_tile(o):
-        dvs[o] = (dv_part[o] + value_sum(o, heads)).astype(BF16)
+        dvs[o] = (dv_part[o] + value_sum(o, heads + early, heads - early)).astype(BF16)
 
     def key_tile(o):
         tile = slot_tile[o]
@@ -318,7 +330,7 @@
         dks[o] = (total * scale).astype(BF16)
 
     def give_values(i, _):
-        group = [peer(group_size * i + 2 + k) for k in range(group_size)]
+        group = [peer(value_group * i + 2 + k) for k in range(value_group)]
         for other in group:
             value_tile(other)
         for other in group:
@@ -327,10 +339,16 @@
 
     value_tile(peer(1))
     dv_copy(peer(1)).start()
-    lax.fori_loop(0, (n_dp - 2) // group_size, give_values, 0)
+    lax.fori_loop(0, (n_dp - 2) // value_group, give_values, 0)
     value_tile(me)
     dv_keep = pltpu.make_async_copy(dvs.at[me], dv_out.at[me], out_sem.at[0])
     dv_keep.start()
+
+    def turn_keys(it, _):
+        kt[it] = kbuf[owners[it // tiles, it % tiles]].astype(F32).T.astype(BF16)
+        return 0
+
+    lax.fori_loop(0, samples * tiles, turn_keys, 0, unroll=4)
 
     def wait_v(i, _):
         landed(vbuf, v_recv, peer(i))
@@ -420,19 +438,27 @@
     dq_keep = pltpu.make_async_copy(dq_stage, dq_out, out_sem.at[2])
     dq_keep.start()
 
-    for b in range(samples):
-        g_copy(b).wait_send()
-
-    def finish(i, _):
+    for h in range(early, heads):
+        g_copy(h).wait_send()
+
+    def finish_values(i, _):
         other = peer(i)
         v_copy(other).wait_send()
         dv_copy(other).wait_send()
-        dk_copy(other).wait_send()
         landed(dv_out, dv_recv, other)
-        landed(dk_out, dk_recv, other)
-        return 0
-
-    lax.fori_loop(1, n_dp, finish, 0)
+        return 0
+
+    def finish_sent(i, _):
+        dk_copy(peer(i)).wait_send()
+        return 0
+
+    def finish_keys(i, _):
+        landed(dk_out, dk_recv, peer(i))
+        return 0
+
+    lax.fori_loop(1, n_dp, finish_values, 0)
+    lax.fori_loop(1, n_dp, finish_sent, 0)
+    lax.fori_loop(1, n_dp, finish_keys, 0)
     dv_keep.wait()
     dk_keep.wait()
     dq_keep.wait()
@@ -493,7 +519,7 @@
         scratch_shapes=[
             pltpu.SMEM((slots,), jnp.int32),
             pltpu.VMEM((2,) + queries.shape, BF16),
-            pltpu.VMEM((2,) + queries.shape, BF16),
+            pltpu.VMEM((2, heads, samples, text, head_dim), BF16),
             pltpu.VMEM((samples, head_dim, rows), BF16),
             pltpu.VMEM(stored, BF16),
             pltpu.VMEM(stored, BF16),
@@ -516,8 +542,10 @@
             pltpu.VMEM((samples, text, width), BF16),
         ]
         + [dma((slots,))] * 8
-        + [dma((samples,))] * 10
-        + [dma((4,)), dma((3,))],
+        + [dma((samples,))] * 2
+        + [dma((heads,))] * 2
+        + [dma((samples,))] * 6
+        + [dma((samples,)), dma((heads,)), dma((2,)), dma((3,))],
         compiler_params=pltpu.CompilerParams(
             collective_id=0, has_side_effects=True, vmem_limit_bytes=56 * 2**20
         ),

time: 116 us -> 115 us (level)
  no operation moved by 1% of the time
where the time goes in v3:
time: 115 us; the launch traced here: 113 us
  Pallas kernels  112 us (97%)
  between operations  1.29 us (1%)
    pallas_call x1, Pallas kernels, shards(): pl.pallas_call(functools.partial(kernel, n_dp), out_shape=results, in_spe...  109 us
    pallas_call x1, Pallas kernels, shards(): pl.pallas_call(place, out_shape=results, in_specs=[hbm] * 3, out_specs=(h...  2.8 us

profile of v3, /device:TPU:40, one launch (start us, length us, event | category | flops | bytes accessed | tf_op | source)
XLA Modules:
  0.0 112.9 jit_solution(13661421117728992913)
XLA Ops:
  1.3 108.8 %cross_attention_backward.1 = (bf16[4,256,512]{2,1,0:T(8,128)(2,1)}, bf16[16,256,128]{2,1,0:T(8,128)(2,1)}, bf16[16,256,128]{2,1,0:T(8,128)(2,1)}) custom-call(s32[4]{0:T(128)} %counts.1, s32[4]{0:T(128)} %lengths.1, s32[4,4]{1,0:T(4,128)} %owners.1, f32[1]{0:T(128)S(6)} %copy.11.gate, bf16[4,256,512]{2,1,0:T(8,128)(2,1)} %q_hbm.1, ...), custom_call_target="tpu_custom_call" | custom-call | tf_op jit(solution)/shard_map/cross_attention_backward/pallas_call | solution.py:514
  110.1 2.8 %place_results.1 = (bf16[4,256,512]{2,1,0:T(8,128)(2,1)}, bf16[16,256,128]{2,1,0:T(8,128)(2,1)}, bf16[16,256,128]{2,1,0:T(8,128)(2,1)}) custom-call(bf16[4,256,512]{2,1,0:T(8,128)(2,1)} %get-tuple-element.9.dq, bf16[16,256,128]{2,1,0:T(8,128)(2,1)} %get-tuple-element.10.dk, bf16[16,256,128]{2,1,0:T(8,128)(2,1)} %get-tuple-element.11.dv), custom_call_target="tpu_custom_call" | custom-call | tf_op jit(solution)/shard_map/place_results/pallas_call | solution.py:563

commit v4 on v2

--- a/solution.py
+++ b/solution.py
@@ -292,11 +292,6 @@
 
     lax.fori_loop(0, n_dp, start_value, 0, unroll=4)
 
-    def turn_keys(it, _):
-        kt[it] = kbuf[owners[it // tiles, it % tiles]].astype(F32).T.astype(BF16)
-        return 0
-
-    lax.fori_loop(0, samples * tiles, turn_keys, 0, unroll=4)
     def scale_got(b, _):
         g_copy(b).wait_recv()
         scale_grad(1, b)
@@ -331,6 +326,12 @@
     value_tile(me)
     dv_keep = pltpu.make_async_copy(dvs.at[me], dv_out.at[me], out_sem.at[0])
     dv_keep.start()
+
+    def turn_keys(it, _):
+        kt[it] = kbuf[owners[it // tiles, it % tiles]].astype(F32).T.astype(BF16)
+        return 0
+
+    lax.fori_loop(0, samples * tiles, turn_keys, 0, unroll=4)
 
     def wait_v(i, _):
         landed(vbuf, v_recv, peer(i))

time: 116 us -> 115 us (level)
  no operation moved by 1% of the time
where the time goes in v4:
time: 115 us; the launch traced here: 113 us
  Pallas kernels  112 us (97%)
  between operations  1.29 us (1%)
    pallas_call x1, Pallas kernels, shards(): pl.pallas_call(functools.partial(kernel, n_dp), out_shape=results, in_spe...  109 us
    pallas_call x1, Pallas kernels, shards(): pl.pallas_call(place, out_shape=results, in_specs=[hbm] * 3, out_specs=(h...  2.8 us

profile of v4, /device:TPU:40, one launch (start us, length us, event | category | flops | bytes accessed | tf_op | source)
XLA Modules:
  0.0 113.1 jit_solution(592290264145381195)
XLA Ops:
  1.3 109.0 %cross_attention_backward.1 = (bf16[4,256,512]{2,1,0:T(8,128)(2,1)}, bf16[16,256,128]{2,1,0:T(8,128)(2,1)}, bf16[16,256,128]{2,1,0:T(8,128)(2,1)}) custom-call(s32[4]{0:T(128)} %counts.1, s32[4]{0:T(128)} %lengths.1, s32[4,4]{1,0:T(4,128)} %owners.1, f32[1]{0:T(128)S(6)} %copy.11.gate, bf16[4,256,512]{2,1,0:T(8,128)(2,1)} %q_hbm.1, ...), custom_call_target="tpu_custom_call" | custom-call | tf_op jit(solution)/shard_map/cross_attention_backward/pallas_call | solution.py:489
  110.3 2.8 %place_results.1 = (bf16[4,256,512]{2,1,0:T(8,128)(2,1)}, bf16[16,256,128]{2,1,0:T(8,128)(2,1)}, bf16[16,256,128]{2,1,0:T(8,128)(2,1)}) custom-call(bf16[4,256,512]{2,1,0:T(8,128)(2,1)} %get-tuple-element.9.dq, bf16[16,256,128]{2,1,0:T(8,128)(2,1)} %get-tuple-element.10.dk, bf16[16,256,128]{2,1,0:T(8,128)(2,1)} %get-tuple-element.11.dv), custom_call_target="tpu_custom_call" | custom-call | tf_op jit(solution)/shard_map/place_results/pallas_call | solution.py:536
